TPU v7x, 256 devices: a whole 4x4x8 slice. The times are simulated.
256 devices in a mesh: frame: 16 (over x_lo, z), patch: 16 (over x_hi, y, core).
Axes of the slice: x: 4 (x_hi: 2, x_lo: 2; x = x_hi * 2 + x_lo), y: 4, z: 8, core: 2. Of those that a mesh axis runs over, the one named last changes fastest.
Arguments:
- frames_in: bfloat16 [512, 256, 1408], P('frame', 'patch'), may hold values from -8 to 8
- ln_gain: float32 [1408], replicated, may hold values from 0.25 to 1.75
- w_query: bfloat16 [1408, 704], replicated, may hold values from -1 to 1
- w_key: bfloat16 [1408, 704], replicated, may hold values from -4 to 4
- w_value: bfloat16 [1408, 704], replicated, may hold values from -0.15625 to 0.15625
- w_out: bfloat16 [704, 1408], replicated, may hold values from -0.21875 to 0.21875
- w_down: bfloat16 [1408, 352], replicated, may hold values from -0.15625 to 0.15625
- conv_kernel: float32 [3, 352], replicated, may hold values from -3 to 3
- w_up: bfloat16 [352, 1408], replicated, may hold values from -0.3125 to 0.3125
Outputs:
- adapted: bfloat16 [512, 256, 1408], P('frame', 'patch')
- pooled: float32 [512, 1408], P('frame', 'patch')
All inputs are finite; a program needn't handle non-finite values.
Results may differ from a plain program's by a relative error of at most 0.017.
Values may be sent and summed in bfloat16 or wider, within the bound.
A program may use at most 192 MiB of HBM per device.

v0:
```python
import math

import jax
import jax.numpy as jnp
from jax import lax
from jax.sharding import PartitionSpec as P

HEAD_SIZE = 88


def with_halo(cells, sides, width):
    for axis, dim in sides:
        count = lax.axis_size(axis)
        ends = count - 1
        head = lax.slice_in_dim(cells, 0, width, axis=dim)
        tail = lax.slice_in_dim(cells, cells.shape[dim] - width, cells.shape[dim], axis=dim)
        cells = jnp.concatenate(
            [
                lax.ppermute(tail, axis, [(i, (i + 1) % count) for i in range(ends)]),
                cells,
                lax.ppermute(head, axis, [((i + 1) % count, i) for i in range(ends)]),
            ],
            axis=dim,
        )
    return cells


def attend(queries, key_rows, value_rows):
    temper = 1.0 / math.sqrt(queries.shape[-1])
    scores = (
        jnp.einsum("fphe,fnhe->fhpn", queries, key_rows, preferred_element_type=jnp.float32)
        * temper
    )
    top = jnp.max(scores, axis=-1, keepdims=True)
    raised = jnp.exp(scores - top)
    totals = jnp.sum(raised, axis=-1, keepdims=True)
    weights = raised.astype(jnp.bfloat16)
    summed = jnp.einsum("fhpn,fnhe->fphe", weights, value_rows, preferred_element_type=jnp.float32)
    return (summed / jnp.transpose(totals, (0, 2, 1, 3))).astype(jnp.bfloat16)


def per_device(frames_in, ln_gain, w_query, w_key, w_value, w_out, w_down, conv_kernel, w_up):
    frame_count, patch_count, width = frames_in.shape
    feature_count = w_query.shape[1]
    head_count = feature_count // HEAD_SIZE
    adapt_width = w_down.shape[1]
    patch_total = patch_count * lax.axis_size("patch")
    wide = frames_in.astype(jnp.float32).reshape(frame_count * patch_count, width)
    average = jnp.mean(wide, axis=-1, keepdims=True)
    variance = jnp.mean((wide - average) ** 2, axis=-1, keepdims=True)
    normed = ((wide - average) * lax.rsqrt(variance + 1e-06) * ln_gain).astype(jnp.bfloat16)
    shape_heads = (frame_count, patch_count, head_count, HEAD_SIZE)
    queries = (
        jnp.dot(normed, w_query, preferred_element_type=jnp.float32)
        .astype(jnp.bfloat16)
        .reshape(shape_heads)
    )
    key_rows = (
        jnp.dot(normed, w_key, preferred_element_type=jnp.float32)
        .astype(jnp.bfloat16)
        .reshape(shape_heads)
    )
    value_rows = (
        jnp.dot(normed, w_value, preferred_element_type=jnp.float32)
        .astype(jnp.bfloat16)
        .reshape(shape_heads)
    )
    stacked = jnp.stack([key_rows, value_rows])
    gathered = lax.all_gather(stacked, "patch", axis=2, tiled=True)
    attended = attend(queries, gathered[0], gathered[1])
    attended = attended.reshape(frame_count * patch_count, feature_count)
    block_out = wide + jnp.dot(attended, w_out, preferred_element_type=jnp.float32)
    reduced = jnp.dot(
        block_out.astype(jnp.bfloat16), w_down, preferred_element_type=jnp.float32
    ).astype(jnp.bfloat16)
    reduced = reduced.reshape(frame_count, patch_count, adapt_width)
    padded = with_halo(reduced, (("frame", 0),), 1)
    blended = (
        padded[:-2] * conv_kernel[0] + padded[1:-1] * conv_kernel[1] + padded[2:] * conv_kernel[2]
    )
    activated = jax.nn.gelu(blended, approximate=True).astype(jnp.bfloat16)
    lifted = jnp.dot(
        activated.reshape(frame_count * patch_count, adapt_width),
        w_up,
        preferred_element_type=jnp.float32,
    )
    full_out = (block_out + lifted).reshape(frame_count, patch_count, width)
    adapted = full_out.astype(jnp.bfloat16)
    partial_sum = jnp.sum(full_out, axis=1) / patch_total
    totals = lax.psum(partial_sum.astype(jnp.bfloat16), "patch").astype(jnp.float32)
    share = width // lax.axis_size("patch")
    pooled = lax.dynamic_slice_in_dim(totals, lax.axis_index("patch") * share, share, 1)
    return (adapted, pooled)


def solution(mesh):
    placed = (P("frame", "patch", None), P(), P(), P(), P(), P(), P(), P(), P())
    return jax.shard_map(
        per_device,
        mesh=mesh,
        in_specs=placed,
        out_specs=(P("frame", "patch", None), P("frame", "patch")),
        check_vma=False,
    )
```

profile of v0, /device:TPU:1, one launch (start us, length us, event | category | flops | bytes accessed | tf_op | source)
XLA Modules:
  0.0 480.5 jit_solution(1973865537273754669)
XLA Ops:
  12.7 2.2 convolution_convert_fusion.1
  14.8 2.2 convolution_convert_fusion.2
  17.0 2.3 copy.26
  19.3 2.3 copy.27
  21.6 3.1 stack_reshape.7
  24.7 3.1 stack_reshape.6
  31.9 4.2 convolution_convert_fusion
  36.1 2.3 copy.30
  38.4 3.1 reshape.62
  41.5 185.7 %all-gather.2.cloned.1.call-done = bf16[2,32,256,8,88]{4,3,1,0,2:T(8,128)(2,1)} async-done(((bf16[2,32,16,8,88]{4,3,1,0,2:T(8,128)(2,1)}), bf16[2,32,256,8,88]{4,3,1,0,2:T(8,128)(2,1)}) %all-gather.2.cloned.1.call-update) | async-done | bytes 23068688 | tf_op jit(solution)/shard_map/all_gather | solution.py:69
  227.1 23.2 %fusion.32 = (bf16[1,32,256,8,88]{4,3,1,0,2:T(8,128)(2,1)}, bf16[1,32,256,8,88]{4,3,1,0,2:T(8,128)(2,1)}) fusion(bf16[2,32,256,8,88]{4,3,1,0,2:T(8,128)(2,1)} %all-gather.2.cloned.1.call-done), kind=kLoop, calls=%fused_computation.50 | loop fusion | bytes 46137344 | tf_op jit(solution)/shard_map/slice | solution.py:70
  250.4 20.9 %copy.37 = bf16[1,32,256,8,88]{2,4,3,1,0:T(8,128)(2,1)} copy(bf16[1,32,256,8,88]{4,3,1,0,2:T(8,128)(2,1)} %get-tuple-element.5) | data formatting | bytes 23068672
  271.3 20.9 %copy.38 = bf16[1,32,256,8,88]{2,4,3,1,0:T(8,128)(2,1)} copy(bf16[1,32,256,8,88]{4,3,1,0,2:T(8,128)(2,1)} %get-tuple-element.6) | data formatting | bytes 23068672
  292.2 6.7 %multiply_reduce_fusion = (f32[32,8,16]{2,1,0:T(8,128)S(1)}, f32[32,8,16,256]{3,2,1,0:T(8,128)S(1)}) fusion(bf16[1,32,256,8,88]{2,4,3,1,0:T(8,128)(2,1)} %copy.38, bf16[32,16,8,88]{3,2,1,0:T(8,128)(2,1)} %reshape.62), kind=kOutput, calls=%fused_computation.5 | convolution fusion | flops 186642432 | bytes 16465920 | tf_op jit(solution)/shard_map/fphe,fnhe->fhpn/dot_general | solution.py:31
  298.9 2.0 copy-done.1
  301.0 2.1 fusion.4
  303.1 12.1 %fusion.10 = bf16[32,16,8,88]{3,1,2,0:T(8,128)(2,1)} fusion(f32[32,16,8]{1,2,0:T(8,128)} %bitcast.53, f32[32,8,16,256]{3,2,1,0:T(8,128)} %copy-done.1, f32[32,8,16]{2,1,0:T(8,128)S(1)} %get-tuple-element.9, bf16[1,32,256,8,88]{2,4,3,1,0:T(8,128)(2,1)} %copy.37), kind=kOutput, calls=%fused_computation.19 | convolution fusion | flops 188416000 | bytes 16482304 | tf_op jit(solution)/shard_map/fhpn,fnhe->fphe/dot_general | solution.py:38
  315.2 2.5 copy.33
  317.7 2.7 reshape.63
  320.4 2.6 convolution_add_fusion.1
  325.4 3.2 collective-permute-start
  330.4 3.5 collective-permute-done.1
  334.4 4.3 bitcast_reduce_fusion
  339.4 132.9 %all-reduce.2.cloned.1.call-done = bf16[32,1408]{1,0:T(8,128)(2,1)} async-done(((bf16[32,1408]{1,0:T(8,128)(2,1)}), bf16[32,1408]{1,0:T(8,128)(2,1)}) %all-reduce.2.cloned.1.call-update) | async-done | bytes 90128 | tf_op jit(solution)/shard_map/psum | solution.py:90
  (43 shorter events, 16.4 us)
Async XLA Ops:
  7.2 313.2 %copy-start = (bf16[704,1408]{1,0:T(8,128)(2,1)S(1)}, bf16[704,1408]{1,0:T(8,128)(2,1)}, u32[]{:S(2)}) copy-start(bf16[704,1408]{1,0:T(8,128)(2,1)} %param.14) | copy-start | bytes 5947396
  7.2 3.9 copy-start.2
  7.2 3.9 copy-start.6
  7.2 219.9 %all-gather.2.cloned.1.call-start = ((), (), s32[]{:S(2)}) async-start(), calls=%async_computation | async-start | bytes 35651584 | tf_op jit(solution)/shard_map/all_gather | solution.py:69
  11.1 1.6 copy-start.8
  12.7 2.2 copy-start.4
  12.7 2.2 copy-start.9
  31.7 440.6 %all-reduce.2.cloned.1.call-start = ((), (), s32[]{:S(2)}) async-start(), calls=%async_computation.1 | async-start | bytes 180224 | tf_op jit(solution)/shard_map/psum | solution.py:90
  298.9 2.1 copy-start.1
  320.4 4.2 copy-start.5
  323.0 1.6 copy-start.3
  324.6 5.4 %copy-start.7 = (f32[3,352]{1,0:T(4,128)S(1)}, f32[3,352]{1,0:T(4,128)}, u32[]{:S(2)}) copy-start(f32[3,352]{1,0:T(4,128)} %param.16) | copy-start | bytes 12676
  325.4 4.9 %collective-permute-start = (bf16[1,16,352]{1,2,0:T(8,128)(2,1)S(1)}, bf16[1,16,352]{1,2,0:T(8,128)(2,1)S(1)}, u32[]{:S(2)}, u32[]{:S(2)}) collective-permute-start(bf16[1,16,352]{1,2,0:T(8,128)(2,1)S(1)} %get-tuple-element.7), channel_id=1, source_target_pairs={{0,16},{16,32},{32,48},{48,64},{64,80},{80,96},{96,112},{112,128},... | collective-permute-start | bytes 33800 | tf_op jit(solution)/shard_map/ppermute | solution.py:19
  328.6 5.3 %collective-permute-start.1 = (bf16[1,16,352]{1,2,0:T(8,128)(2,1)S(1)}, bf16[1,16,352]{1,2,0:T(8,128)(2,1)S(1)}, u32[]{:S(2)}, u32[]{:S(2)}) collective-permute-start(bf16[1,16,352]{1,2,0:T(8,128)(2,1)S(1)} %get-tuple-element.8), channel_id=1, source_target_pairs={{16,0},{32,16},{48,32},{64,48},{80,64},{96,80},{112,96},{128,112},... | collective-permute-start | bytes 33800 | tf_op jit(solution)/shard_map/ppermute | solution.py:21
Sparse Core Ops, SparseCore 0:
  31.8 195.2 all-gather.1
  339.5 132.7 all-reduce.1
where the time goes:
time: 483 us; the launch traced here: 481 us
  waiting for transfers between devices  322 us (67%)
  local copies, waits for them, and re-layouts  93.6 us (19%)
  matrix products  34.9 us (7%)
  between operations  14.2 us (3%)
  other arithmetic  10.8 us (2%)
    all_gather x1, waiting for transfers between devices, per_device(): gathered = lax.all_gather(stacked, 'patch', axis=2, tiled=True)  186 us
    psum x1, waiting for transfers between devices, per_device(): lax.psum(partial_sum.astype(jnp.bfloat16), 'patch').astype(jnp.float32)  133 us
    unnamed x22, local copies, waits for them, and re-layouts  46.5 us
    slice x1, local copies, waits for them, and re-layouts, per_device(): attended = attend(queries, gathered[0], gathered[1])  23.2 us
    dot_general x1, matrix products, attend(): jnp.einsum('fhpn,fnhe->fphe', weights, value_rows, preferred_element_type...  12.1 us
  transfers between devices with their start and end apart: 4, of which 4 were waited for; matrix products, arithmetic and copies ran while one was open for 2% of the time, Pallas kernels for 0%

commit v1 on v0

v1 whole, which is shorter than its diff:
```python
import functools
import math

import jax
import jax.numpy as jnp
from jax import lax
from jax.experimental import pallas as pl
from jax.experimental.pallas import tpu as pltpu
from jax.sharding import PartitionSpec as P

HEAD_SIZE = 88
LANES = 128
MESH = pl.DeviceIdType.MESH
F32 = jnp.float32
BF16 = jnp.bfloat16


def dot(a, b):
    return jnp.dot(a, b, preferred_element_type=F32)


def dot_turned(a, b):
    return lax.dot_general(a, b, (((1,), (1,)), ((), ())), preferred_element_type=F32)


def layer_kernel(
    n, ring,
    x_ref, gain_ref, wq_ref, wk_ref, wv_ref, wo_ref, wd_ref, conv_ref, wu_ref,
    adapted_ref, pooled_ref,
    home, xr, normed, q, k, v, acc, att, ah, wq, wk, wv, wo, wd, wu,
    block, red, halo, part, psend, precv,
    load_sem, own_sem, x_send, x_recv, a_send, a_recv, h_send, h_recv, p_send, p_recv,
):
    f, p = lax.axis_index("frame"), lax.axis_index("patch")
    patches, width = x_ref.shape[1], x_ref.shape[2]
    features = wq.shape[0]
    tokens = n * patches
    half = n // 2
    quarter = half * patches

    def start_of(c, u):
        return c * half + u * ((n + half) * (1 - c) + half * c)

    def frame_of(c, j):
        u = j // half
        return start_of(c, u) + j - u * half

    loads = [
        pltpu.make_async_copy(src, dst, load_sem.at[i])
        for i, (src, dst) in enumerate(
            [(wq_ref, wq), (wk_ref, wk), (wv_ref, wv), (wo_ref, wo), (wd_ref, wd), (wu_ref, wu)]
        )
    ]

    def own_x(c):
        return pltpu.make_async_copy(x_ref.at[frame_of(c, p)], xr.at[c, p], own_sem.at[c])

    def own_att(c):
        return pltpu.make_async_copy(att.at[c, p], ah.at[c, p], own_sem.at[2 + c])

    def home_copy(c, u):
        return pltpu.make_async_copy(
            x_ref.at[pl.ds(start_of(c, u), half)],
            home.at[c, pl.ds(u * half, half)],
            own_sem.at[4 + 2 * c + u],
        )

    def x_copy(c, i):
        d = lax.rem(p + i, n)
        return pltpu.make_async_remote_copy(
            x_ref.at[frame_of(c, d)], xr.at[c, p], x_send.at[c, i], x_recv.at[c, p],
            device_id=(f, d), device_id_type=MESH,
        )

    def x_arrival(c, s):
        return pltpu.make_async_remote_copy(
            x_ref.at[0], xr.at[c, s], x_send.at[c, 0], x_recv.at[c, s],
            device_id=(f, s), device_id_type=MESH,
        )

    def a_copy(c, i):
        d = lax.rem(p + i, n)
        return pltpu.make_async_remote_copy(
            att.at[c, d], ah.at[c, p], a_send.at[c, i], a_recv.at[c, p],
            device_id=(f, d), device_id_type=MESH,
        )

    def a_arrival(c, s):
        return pltpu.make_async_remote_copy(
            att.at[c, 0], ah.at[c, s], a_send.at[c, 0], a_recv.at[c, s],
            device_id=(f, s), device_id_type=MESH,
        )

    before, after = lax.rem(f + ring - 1, ring), lax.rem(f + 1, ring)
    last = 2 * n
    to_after = pltpu.make_async_remote_copy(
        red.at[last], halo.at[0], h_send.at[0], h_recv.at[0],
        device_id=(after, p), device_id_type=MESH,
    )
    to_before = pltpu.make_async_remote_copy(
        red.at[1], halo.at[1], h_send.at[1], h_recv.at[1],
        device_id=(before, p), device_id_type=MESH,
    )

    def p_copy(i):
        d = lax.rem(p + i, n)
        return pltpu.make_async_remote_copy(
            psend.at[d], precv.at[p], p_send.at[i], p_recv.at[p],
            device_id=(f, d), device_id_type=MESH,
        )

    def p_arrival(s):
        return pltpu.make_async_remote_copy(
            psend.at[0], precv.at[s], p_send.at[0], p_recv.at[s],
            device_id=(f, s), device_id_type=MESH,
        )

    barrier = pltpu.get_barrier_semaphore()

    @pl.loop(1, n)
    def _(i):
        pl.semaphore_signal(barrier, inc=1, device_id=(f, lax.rem(p + i, n)), device_id_type=MESH)

    for side in (before, after):
        pl.semaphore_signal(barrier, inc=1, device_id=(side, p), device_id_type=MESH)

    own_x(0).start()
    for load in loads[:3]:
        load.start()
    own_x(1).start()
    for c in range(2):
        for u in range(2):
            home_copy(c, u).start()
    for load in loads[3:]:
        load.start()

    pl.semaphore_wait(barrier, n + 1)

    @pl.loop(1, n)
    def _(i):
        x_copy(0, i).start()

    def attention():
        lane = lax.broadcasted_iota(jnp.int32, (1, 2 * LANES), 1)
        scale = math.log2(math.e) / math.sqrt(HEAD_SIZE)
        for h in range(features // HEAD_SIZE):
            low = h * HEAD_SIZE
            a = low // LANES * LANES
            b = min(-(-(low + HEAD_SIZE) // LANES) * LANES, features)
            inside = (lane[:, : b - a] >= low - a) & (lane[:, : b - a] < low - a + HEAD_SIZE)
            mine = inside.astype(F32).astype(BF16)
            scores = dot_turned(q[:, a:b] * mine, k[:, a:b])
            top = jnp.max(scores, axis=-1, keepdims=True)
            raised = jnp.exp2((scores - top) * scale)
            totals = jnp.sum(raised, axis=-1, keepdims=True)
            summed = dot(raised.astype(BF16), v[:, a:b]) / totals
            acc[:, a:b] = jnp.where(inside, summed, acc[:, a:b])

    @pl.loop(0, 2)
    def _(c):
        @pl.loop(0, n)
        def _(i):
            s = lax.rem(p + n - i, n)

            @pl.when(i == 0)
            def _():
                own_x(c).wait()

            @pl.when(i > 0)
            def _():
                x_arrival(c, s).wait_recv()

                @pl.when(c == 0)
                def _():
                    x_copy(1, i).start()

            wide = xr[c, s].astype(F32)
            centered = wide - jnp.mean(wide, axis=-1, keepdims=True)
            variance = jnp.mean(centered * centered, axis=-1, keepdims=True)
            rows = pl.ds(pl.multiple_of(s * patches, patches), patches)
            normed[rows, :] = (centered * lax.rsqrt(variance + 1e-06) * gain_ref[...].reshape(1, width)).astype(BF16)

        @pl.when(c == 0)
        def _():
            for load in loads[:3]:
                load.wait()

        @pl.when(c == 1)
        def _():
            @pl.loop(1, n)
            def _(i):
                a_copy(0, i).start()

        for dst, weight in ((q, wq), (k, wk), (v, wv)):
            dst[...] = dot_turned(normed[...], weight[...]).astype(BF16)
        attention()
        att[c] = acc[...].astype(BF16).reshape(n, patches, features)
        own_att(c).start()

    @pl.loop(1, n)
    def _(i):
        a_copy(1, i).start()

    for load in loads[3:]:
        load.wait()

    @pl.loop(0, 2)
    def _(c):
        for u in range(2):
            home_copy(c, u).wait()
        own_att(c).wait()

        @pl.loop(1, n)
        def _(i):
            a_arrival(c, lax.rem(p + n - i, n)).wait_recv()

        here = dot(ah[c].reshape(tokens, features), wo[...])
        here += home[c].reshape(tokens, width).astype(F32)
        block[c] = here
        reduced = dot_turned(here.astype(BF16), wd[...]).astype(BF16)
        reduced = reduced.reshape(n, patches, wd.shape[0])
        for u in range(2):
            red[pl.ds(1 + start_of(c, u), half)] = reduced[u * half : (u + 1) * half]

        @pl.when(c == 0)
        def _():
            to_after.start()
            to_before.start()

    to_after.wait()
    to_before.wait()
    red[0] = jnp.where(f > 0, halo[0].astype(F32), 0.0).astype(BF16)
    red[last + 1] = jnp.where(f < ring - 1, halo[1].astype(F32), 0.0).astype(BF16)

    @pl.loop(0, 4)
    def _(j):
        c, u = j // 2, j % 2
        start = start_of(c, u)
        taps = [red[pl.ds(start + t, half)].astype(F32) * conv_ref[t : t + 1, :] for t in range(3)]
        activated = jax.nn.gelu(taps[0] + taps[1] + taps[2], approximate=True).astype(BF16)
        rows = pl.ds(pl.multiple_of(u * quarter, quarter), quarter)
        full = block[c, rows, :] + dot(activated.reshape(quarter, wu.shape[0]), wu[...])
        full = full.reshape(half, patches, width)
        part[pl.ds(pl.multiple_of(start, half), half), :] = jnp.sum(full, axis=1) / (n * patches)
        adapted_ref[pl.ds(start, half)] = full.astype(BF16)

    share = width // n
    for d in range(n):
        psend[d, :, :share] = part[:, d * share : (d + 1) * share].astype(BF16)

    @pl.loop(1, n)
    def _(i):
        p_copy(i).start()

    precv[p] = psend[p]

    @pl.loop(1, n)
    def _(i):
        p_arrival(lax.rem(p + n - i, n)).wait_recv()

    pooled_ref[...] = jnp.sum(precv[...].astype(F32), axis=0)[:, :share]

    @pl.loop(1, n)
    def _(i):
        for c in range(2):
            x_copy(c, i).wait_send()
            a_copy(c, i).wait_send()
        p_copy(i).wait_send()


def per_device(n, ring, frames_in, ln_gain, w_query, w_key, w_value, w_out, w_down, conv_kernel, w_up):
    frames, patches, width = frames_in.shape
    features, adapt = w_query.shape[1], w_down.shape[1]
    tokens = n * patches
    share = width // n
    any_spec = pl.BlockSpec(memory_space=pltpu.HBM)
    vmem_spec = pl.BlockSpec(memory_space=pltpu.VMEM)
    dma = pltpu.SemaphoreType.DMA
    padded = -(-share // LANES) * LANES
    return pl.pallas_call(
        functools.partial(layer_kernel, n, ring),
        out_shape=(
            jax.ShapeDtypeStruct((frames, patches, width), BF16),
            jax.ShapeDtypeStruct((frames, share), F32),
        ),
        in_specs=[any_spec, vmem_spec] + [any_spec] * 5 + [vmem_spec, any_spec],
        out_specs=(vmem_spec, vmem_spec),
        scratch_shapes=[
            pltpu.VMEM((2, n, patches, width), BF16),
            pltpu.VMEM((2, n, patches, width), BF16),
            pltpu.VMEM((tokens, width), BF16),
            pltpu.VMEM((tokens, features), BF16),
            pltpu.VMEM((tokens, features), BF16),
            pltpu.VMEM((tokens, features), BF16),
            pltpu.VMEM((tokens, features), F32),
            pltpu.VMEM((2, n, patches, features), BF16),
            pltpu.VMEM((2, n, patches, features), BF16),
            pltpu.VMEM(w_query.shape[::-1], BF16),
            pltpu.VMEM(w_key.shape[::-1], BF16),
            pltpu.VMEM(w_value.shape[::-1], BF16),
            pltpu.VMEM(w_out.shape, BF16),
            pltpu.VMEM(w_down.shape[::-1], BF16),
            pltpu.VMEM(w_up.shape, BF16),
            pltpu.VMEM((2, tokens, width), F32),
            pltpu.VMEM((frames + 2, patches, adapt), BF16),
            pltpu.VMEM((2, patches, adapt), BF16),
            pltpu.VMEM((frames, width), F32),
            pltpu.VMEM((n, frames, padded), BF16),
            pltpu.VMEM((n, frames, padded), BF16),
            dma((6,)), dma((8,)), dma((2, n)), dma((2, n)), dma((2, n)), dma((2, n)),
            dma((2,)), dma((2,)), dma((n,)), dma((n,)),
        ],
        compiler_params=pltpu.CompilerParams(
            collective_id=0, has_side_effects=True, vmem_limit_bytes=48 * 1024 * 1024
        ),
    )(
        frames_in, ln_gain, w_query.T, w_key.T, w_value.T, w_out, w_down.T, conv_kernel, w_up,
    )


def solution(mesh):
    placed = (P("frame", "patch", None), P(), P(), P(), P(), P(), P(), P(), P())
    return jax.shard_map(
        functools.partial(per_device, mesh.shape["patch"], mesh.shape["frame"]),
        mesh=mesh,
        in_specs=placed,
        out_specs=(P("frame", "patch", None), P("frame", "patch")),
        check_vma=False,
    )
```

time: 483 us -> 61.9 us (0.13)
  waiting for transfers between devices: 322 us -> 0 us
  local copies, waits for them, and re-layouts: 93.6 us -> 6.86 us
  Pallas kernels: 0 us -> 54.1 us
  matrix products: 34.9 us -> 0 us
  between operations: 14.2 us -> 0.65 us
  other arithmetic: 10.8 us -> 0 us
    all_gather x1 -> x0, waiting for transfers between devices: 186 us -> none  [per_device(): gathered = lax.all_gather(stacked, 'patch', axis=2, tiled=True)]
    psum x1 -> x0, waiting for transfers between devices: 133 us -> none  [per_device(): lax.psum(partial_sum.astype(jnp.bfloat16), 'patch').astype(jnp.float32)]
    pallas_call x0 -> x1, Pallas kernels: none -> 54.1 us  [per_device(): pl.pallas_call(functools.partial(layer_kernel, n, ring), out_shape=(jax.S...]
    unnamed x22 -> x12, local copies, waits for them, and re-layouts: 46.5 us -> 6.86 us
    dot_general x8 -> x0, matrix products: 34.9 us -> none  [the longest x1 12.1 us: attend(): jnp.einsum('fhpn,fnhe->fphe', weights, value_rows, preferred_element_type...]
    slice x3 -> x0, local copies, waits for them, and re-layouts: 23.4 us -> none  [the longest x1 23.2 us: per_device(): attended = attend(queries, gathered[0], gathered[1])]
    convert_element_type x5 -> x0, local copies, waits for them, and re-layouts: 9.57 us -> none  [the longest x1 2.49 us: attend(): return (summed / jnp.transpose(totals, (0, 2, 1, 3))).astype(jnp.bfloat16)]
    another operation x3 -> x0, local copies, waits for them, and re-layouts: 8.06 us -> none  [per_device(): stacked = jnp.stack([key_rows, value_rows])]
  transfers between devices with their start and end apart: 4 -> 0, of which waited for: 4 -> 0; matrix products, arithmetic and copies ran while one was open for 2% -> 0% of each run, Pallas kernels for 0% -> 0%
where the time goes in v1:
time: 61.9 us; the launch traced here: 61.7 us
  Pallas kernels  54.1 us (87%)
  local copies, waits for them, and re-layouts  6.86 us (11%)
  between operations  0.65 us (1%)
    pallas_call x1, Pallas kernels, per_device(): pl.pallas_call(functools.partial(layer_kernel, n, ring), out_shape=(jax.S...  54.1 us
    unnamed x12, local copies, waits for them, and re-layouts  6.86 us

profile of v1, /device:TPU:1, one launch (start us, length us, event | category | flops | bytes accessed | tf_op | source)
XLA Modules:
  0.0 61.7 jit_solution(1188473154955075826)
XLA Ops:
  0.6 0.0 copy-start
  0.6 1.4 %copy-done = bf16[32,16,1408]{2,1,0:T(8,128)(2,1)S(1)} copy-done((bf16[32,16,1408]{2,1,0:T(8,128)(2,1)S(1)}, bf16[32,16,1408]{2,1,0:T(8,128)(2,1)}, u32[]{:S(2)}) %copy-start) | copy-done | bytes 1441816
  2.0 0.0 copy-start.1
  2.0 1.2 %copy-done.1 = bf16[1408,352]{0,1:T(8,128)(2,1)S(1)} copy-done((bf16[1408,352]{0,1:T(8,128)(2,1)S(1)}, bf16[1408,352]{0,1:T(8,128)(2,1)}, u32[]{:S(2)}) %copy-start.1) | copy-done | bytes 991256
  3.2 0.0 copy-start.2
  3.2 1.2 %copy-done.2 = bf16[352,1408]{1,0:T(8,128)(2,1)S(1)} copy-done((bf16[352,1408]{1,0:T(8,128)(2,1)S(1)}, bf16[352,1408]{1,0:T(8,128)(2,1)}, u32[]{:S(2)}) %copy-start.2) | copy-done | bytes 991256
  4.4 0.0 copy-start.3
  4.4 0.7 %copy-done.3 = f32[1408]{0:T(1024)S(1)} copy-done((f32[1408]{0:T(1024)S(1)}, f32[1408]{0:T(1024)}, u32[]{:S(2)}) %copy-start.3) | copy-done | bytes 5656
  5.1 0.0 copy-start.4
  5.1 0.7 %copy-done.4 = f32[3,352]{1,0:T(4,128)S(1)} copy-done((f32[3,352]{1,0:T(4,128)S(1)}, f32[3,352]{1,0:T(4,128)}, u32[]{:S(2)}) %copy-start.4) | copy-done | bytes 4248
  5.8 54.1 %shard_map.104 = (bf16[32,16,1408]{2,1,0:T(8,128)(2,1)S(1)}, f32[32,88]{1,0:T(8,128)S(1)}) custom-call(bf16[32,16,1408]{2,1,0:T(8,128)(2,1)S(1)} %copy-done, f32[1408]{0:T(1024)S(1)} %copy-done.3, bf16[704,1408]{1,0:T(8,128)(2,1)} %bitcast.5, bf16[704,1408]{1,0:T(8,128)(2,1)} %bitcast.6, bf16[704,1408]{1,0:T(8,128)(2,1)} %bitcast.7, ...), custom_call_target="tpu_custom_call" | custom-call | tf_op jit(solution)/shard_map/pallas_call | solution.py:280
  59.9 1.1 %copy.13 = bf16[32,16,1408]{2,1,0:T(8,128)(2,1)} copy(bf16[32,16,1408]{2,1,0:T(8,128)(2,1)S(1)} %get-tuple-element.4) | data formatting | bytes 2883584
  61.0 0.6 copy.14
Async XLA Ops:
  0.6 1.4 %copy-start = (bf16[32,16,1408]{2,1,0:T(8,128)(2,1)S(1)}, bf16[32,16,1408]{2,1,0:T(8,128)(2,1)}, u32[]{:S(2)}) copy-start(bf16[32,16,1408]{2,1,0:T(8,128)(2,1)} %x_ref.1) | copy-start | bytes 4325380
  2.0 1.2 %copy-start.1 = (bf16[1408,352]{0,1:T(8,128)(2,1)S(1)}, bf16[1408,352]{0,1:T(8,128)(2,1)}, u32[]{:S(2)}) copy-start(bf16[1408,352]{0,1:T(8,128)(2,1)} %param.15) | copy-start | bytes 2973700
  3.2 1.2 %copy-start.2 = (bf16[352,1408]{1,0:T(8,128)(2,1)S(1)}, bf16[352,1408]{1,0:T(8,128)(2,1)}, u32[]{:S(2)}) copy-start(bf16[352,1408]{1,0:T(8,128)(2,1)} %wu_ref.1) | copy-start | bytes 2973700
  4.4 0.7 %copy-start.3 = (f32[1408]{0:T(1024)S(1)}, f32[1408]{0:T(1024)}, u32[]{:S(2)}) copy-start(f32[1408]{0:T(1024)} %gain_ref.1) | copy-start | bytes 16900
  5.1 0.7 %copy-start.4 = (f32[3,352]{1,0:T(4,128)S(1)}, f32[3,352]{1,0:T(4,128)}, u32[]{:S(2)}) copy-start(f32[3,352]{1,0:T(4,128)} %conv_ref.1) | copy-start | bytes 12676

commit v2 on v1

--- a/solution.py
+++ b/solution.py
@@ -9,6 +9,7 @@
 from jax.sharding import PartitionSpec as P
 
 HEAD_SIZE = 88
+SLOTS = 4
 LANES = 128
 MESH = pl.DeviceIdType.MESH
 F32 = jnp.float32
@@ -36,7 +37,6 @@
     features = wq.shape[0]
     tokens = n * patches
     half = n // 2
-    quarter = half * patches
 
     def start_of(c, u):
         return c * half + u * ((n + half) * (1 - c) + half * c)
@@ -53,35 +53,24 @@
     ]
 
     def own_x(c):
-        return pltpu.make_async_copy(x_ref.at[frame_of(c, p)], xr.at[c, p], own_sem.at[c])
+        return pltpu.make_async_copy(home.at[frame_of(c, p)], xr.at[c, 0], own_sem.at[c])
 
     def own_att(c):
-        return pltpu.make_async_copy(att.at[c, p], ah.at[c, p], own_sem.at[2 + c])
-
-    def home_copy(c, u):
-        return pltpu.make_async_copy(
-            x_ref.at[pl.ds(start_of(c, u), half)],
-            home.at[c, pl.ds(u * half, half)],
-            own_sem.at[4 + 2 * c + u],
-        )
+        return pltpu.make_async_copy(att.at[c, 0], ah.at[c, p], own_sem.at[2 + c])
+
+    home_copy = pltpu.make_async_copy(x_ref, home, own_sem.at[4])
 
     def x_copy(c, i):
         d = lax.rem(p + i, n)
         return pltpu.make_async_remote_copy(
-            x_ref.at[frame_of(c, d)], xr.at[c, p], x_send.at[c, i], x_recv.at[c, p],
+            home.at[frame_of(c, d)], xr.at[c, i], x_send.at[c, i], x_recv.at[c, i],
             device_id=(f, d), device_id_type=MESH,
         )
 
-    def x_arrival(c, s):
+    def a_copy(c, i):
+        d = lax.rem(p + n - i, n)
         return pltpu.make_async_remote_copy(
-            x_ref.at[0], xr.at[c, s], x_send.at[c, 0], x_recv.at[c, s],
-            device_id=(f, s), device_id_type=MESH,
-        )
-
-    def a_copy(c, i):
-        d = lax.rem(p + i, n)
-        return pltpu.make_async_remote_copy(
-            att.at[c, d], ah.at[c, p], a_send.at[c, i], a_recv.at[c, p],
+            att.at[c, i], ah.at[c, p], a_send.at[c, i], a_recv.at[c, p],
             device_id=(f, d), device_id_type=MESH,
         )
 
@@ -105,16 +94,11 @@
     def p_copy(i):
         d = lax.rem(p + i, n)
         return pltpu.make_async_remote_copy(
-            psend.at[d], precv.at[p], p_send.at[i], p_recv.at[p],
+            psend.at[d], precv.at[i], p_send.at[i], p_recv.at[i],
             device_id=(f, d), device_id_type=MESH,
         )
 
-    def p_arrival(s):
-        return pltpu.make_async_remote_copy(
-            psend.at[0], precv.at[s], p_send.at[0], p_recv.at[s],
-            device_id=(f, s), device_id_type=MESH,
-        )
-
+    home_copy.start()
     barrier = pltpu.get_barrier_semaphore()
 
     @pl.loop(1, n)
@@ -124,21 +108,20 @@
     for side in (before, after):
         pl.semaphore_signal(barrier, inc=1, device_id=(side, p), device_id_type=MESH)
 
-    own_x(0).start()
-    for load in loads[:3]:
+    for load in loads:
         load.start()
-    own_x(1).start()
+    home_copy.wait()
     for c in range(2):
-        for u in range(2):
-            home_copy(c, u).start()
-    for load in loads[3:]:
-        load.start()
-
+        own_x(c).start()
     pl.semaphore_wait(barrier, n + 1)
 
     @pl.loop(1, n)
     def _(i):
         x_copy(0, i).start()
+
+    @pl.loop(1, n)
+    def _(i):
+        x_copy(1, i).start()
 
     def attention():
         lane = lax.broadcasted_iota(jnp.int32, (1, 2 * LANES), 1)
@@ -156,40 +139,34 @@
             summed = dot(raised.astype(BF16), v[:, a:b]) / totals
             acc[:, a:b] = jnp.where(inside, summed, acc[:, a:b])
 
+    rows_in = SLOTS * patches
+
     @pl.loop(0, 2)
     def _(c):
-        @pl.loop(0, n)
-        def _(i):
-            s = lax.rem(p + n - i, n)
-
-            @pl.when(i == 0)
-            def _():
-                own_x(c).wait()
-
-            @pl.when(i > 0)
-            def _():
-                x_arrival(c, s).wait_recv()
-
-                @pl.when(c == 0)
+        @pl.loop(0, n // SLOTS)
+        def _(g):
+            for i in range(SLOTS):
+                slot = g * SLOTS + i
+
+                @pl.when(slot == 0)
                 def _():
-                    x_copy(1, i).start()
-
-            wide = xr[c, s].astype(F32)
+                    own_x(c).wait()
+
+                @pl.when(slot > 0)
+                def _():
+                    x_copy(c, slot).wait_recv()
+
+            wide = xr[c, pl.ds(g * SLOTS, SLOTS)].reshape(rows_in, width).astype(F32)
             centered = wide - jnp.mean(wide, axis=-1, keepdims=True)
             variance = jnp.mean(centered * centered, axis=-1, keepdims=True)
-            rows = pl.ds(pl.multiple_of(s * patches, patches), patches)
-            normed[rows, :] = (centered * lax.rsqrt(variance + 1e-06) * gain_ref[...].reshape(1, width)).astype(BF16)
+            gain = gain_ref[...].reshape(1, width)
+            rows = pl.ds(pl.multiple_of(g * rows_in, rows_in), rows_in)
+            normed[rows, :] = (centered * lax.rsqrt(variance + 1e-06) * gain).astype(BF16)
 
         @pl.when(c == 0)
         def _():
             for load in loads[:3]:
                 load.wait()
-
-        @pl.when(c == 1)
-        def _():
-            @pl.loop(1, n)
-            def _(i):
-                a_copy(0, i).start()
 
         for dst, weight in ((q, wq), (k, wk), (v, wv)):
             dst[...] = dot_turned(normed[...], weight[...]).astype(BF16)
@@ -197,17 +174,14 @@
         att[c] = acc[...].astype(BF16).reshape(n, patches, features)
         own_att(c).start()
 
-    @pl.loop(1, n)
-    def _(i):
-        a_copy(1, i).start()
+        @pl.loop(1, n)
+        def _(i):
+            a_copy(c, i).start()
 
     for load in loads[3:]:
         load.wait()
 
-    @pl.loop(0, 2)
-    def _(c):
-        for u in range(2):
-            home_copy(c, u).wait()
+    def come_home(c):
         own_att(c).wait()
 
         @pl.loop(1, n)
@@ -215,34 +189,44 @@
             a_arrival(c, lax.rem(p + n - i, n)).wait_recv()
 
         here = dot(ah[c].reshape(tokens, features), wo[...])
-        here += home[c].reshape(tokens, width).astype(F32)
-        block[c] = here
+        tokens_in = jnp.concatenate([home[start_of(c, u) : start_of(c, u) + half] for u in range(2)])
+        here += tokens_in.reshape(tokens, width).astype(F32)
         reduced = dot_turned(here.astype(BF16), wd[...]).astype(BF16)
+        here = here.reshape(n, patches, width)
         reduced = reduced.reshape(n, patches, wd.shape[0])
         for u in range(2):
-            red[pl.ds(1 + start_of(c, u), half)] = reduced[u * half : (u + 1) * half]
-
-        @pl.when(c == 0)
-        def _():
-            to_after.start()
-            to_before.start()
-
+            start = start_of(c, u)
+            block[start : start + half] = here[u * half : (u + 1) * half]
+            red[1 + start : 1 + start + half] = reduced[u * half : (u + 1) * half]
+
+    def adapter(spans):
+        taps = [
+            jnp.concatenate([red[start + t : stop + t] for start, stop in spans]).astype(F32)
+            * conv_ref[t : t + 1, :]
+            for t in range(3)
+        ]
+        activated = jax.nn.gelu(taps[0] + taps[1] + taps[2], approximate=True).astype(BF16)
+        count = activated.shape[0]
+        lifted = dot(activated.reshape(count * patches, wu.shape[0]), wu[...])
+        lifted = lifted.reshape(count, patches, width)
+        at = 0
+        for start, stop in spans:
+            full = block[start:stop] + lifted[at : at + stop - start]
+            part[start:stop, :] = jnp.sum(full, axis=1) / (n * patches)
+            adapted_ref[start:stop] = full.astype(BF16)
+            at += stop - start
+
+    come_home(0)
+    to_after.start()
+    to_before.start()
+    adapter([(1, half - 1), (last - half + 1, last - 1)])
+
+    come_home(1)
     to_after.wait()
     to_before.wait()
     red[0] = jnp.where(f > 0, halo[0].astype(F32), 0.0).astype(BF16)
     red[last + 1] = jnp.where(f < ring - 1, halo[1].astype(F32), 0.0).astype(BF16)
-
-    @pl.loop(0, 4)
-    def _(j):
-        c, u = j // 2, j % 2
-        start = start_of(c, u)
-        taps = [red[pl.ds(start + t, half)].astype(F32) * conv_ref[t : t + 1, :] for t in range(3)]
-        activated = jax.nn.gelu(taps[0] + taps[1] + taps[2], approximate=True).astype(BF16)
-        rows = pl.ds(pl.multiple_of(u * quarter, quarter), quarter)
-        full = block[c, rows, :] + dot(activated.reshape(quarter, wu.shape[0]), wu[...])
-        full = full.reshape(half, patches, width)
-        part[pl.ds(pl.multiple_of(start, half), half), :] = jnp.sum(full, axis=1) / (n * patches)
-        adapted_ref[pl.ds(start, half)] = full.astype(BF16)
+    adapter([(0, 1), (half - 1, last - half + 1), (last - 1, last)])
 
     share = width // n
     for d in range(n):
@@ -252,19 +236,22 @@
     def _(i):
         p_copy(i).start()
 
-    precv[p] = psend[p]
-
-    @pl.loop(1, n)
-    def _(i):
-        p_arrival(lax.rem(p + n - i, n)).wait_recv()
-
-    pooled_ref[...] = jnp.sum(precv[...].astype(F32), axis=0)[:, :share]
+    precv[0] = psend[p]
 
     @pl.loop(1, n)
     def _(i):
         for c in range(2):
             x_copy(c, i).wait_send()
             a_copy(c, i).wait_send()
+
+    @pl.loop(1, n)
+    def _(i):
+        p_copy(i).wait_recv()
+
+    pooled_ref[...] = jnp.sum(precv[...].astype(F32), axis=0)[:, :share]
+
+    @pl.loop(1, n)
+    def _(i):
         p_copy(i).wait_send()
 
 
@@ -286,7 +273,7 @@
         in_specs=[any_spec, vmem_spec] + [any_spec] * 5 + [vmem_spec, any_spec],
         out_specs=(vmem_spec, vmem_spec),
         scratch_shapes=[
-            pltpu.VMEM((2, n, patches, width), BF16),
+            pltpu.VMEM((frames, patches, width), BF16),
             pltpu.VMEM((2, n, patches, width), BF16),
             pltpu.VMEM((tokens, width), BF16),
             pltpu.VMEM((tokens, features), BF16),
@@ -301,17 +288,17 @@
             pltpu.VMEM(w_out.shape, BF16),
             pltpu.VMEM(w_down.shape[::-1], BF16),
             pltpu.VMEM(w_up.shape, BF16),
-            pltpu.VMEM((2, tokens, width), F32),
+            pltpu.VMEM((frames, patches, width), F32),
             pltpu.VMEM((frames + 2, patches, adapt), BF16),
             pltpu.VMEM((2, patches, adapt), BF16),
             pltpu.VMEM((frames, width), F32),
             pltpu.VMEM((n, frames, padded), BF16),
             pltpu.VMEM((n, frames, padded), BF16),
-            dma((6,)), dma((8,)), dma((2, n)), dma((2, n)), dma((2, n)), dma((2, n)),
+            dma((6,)), dma((5,)), dma((2, n)), dma((2, n)), dma((2, n)), dma((2, n)),
             dma((2,)), dma((2,)), dma((n,)), dma((n,)),
         ],
         compiler_params=pltpu.CompilerParams(
-            collective_id=0, has_side_effects=True, vmem_limit_bytes=48 * 1024 * 1024
+            collective_id=0, has_side_effects=True, vmem_limit_bytes=60 * 1024 * 1024
         ),
     )(
         frames_in, ln_gain, w_query.T, w_key.T, w_value.T, w_out, w_down.T, conv_kernel, w_up,

time: 61.9 us -> 55.1 us (0.89)
  local copies, waits for them, and re-layouts: 6.86 us -> 3.18 us
  Pallas kernels: 54.1 us -> 51.1 us
    unnamed x12 -> x4, local copies, waits for them, and re-layouts: 6.86 us -> 3.18 us
    pallas_call x1, Pallas kernels: 54.1 us -> 51.1 us  [per_device(): pl.pallas_call(functools.partial(layer_kernel, n, ring), out_shape=(jax.S...]
where the time goes in v2:
time: 55.1 us; the launch traced here: 55 us
  Pallas kernels  51.1 us (93%)
  local copies, waits for them, and re-layouts  3.18 us (6%)
  between operations  0.65 us (1%)
    pallas_call x1, Pallas kernels, per_device(): pl.pallas_call(functools.partial(layer_kernel, n, ring), out_shape=(jax.S...  51.1 us
    unnamed x4, local copies, waits for them, and re-layouts  3.18 us

profile of v2, /device:TPU:1, one launch (start us, length us, event | category | flops | bytes accessed | tf_op | source)
XLA Modules:
  0.0 55.0 jit_solution(10865156257132771530)
XLA Ops:
  0.6 51.1 %shard_map.104 = (bf16[32,16,1408]{2,1,0:T(8,128)(2,1)}, f32[32,88]{1,0:T(8,128)}) custom-call(bf16[32,16,1408]{2,1,0:T(8,128)(2,1)} %x_ref.1, f32[1408]{0:T(1024)} %gain_ref.1, bf16[704,1408]{1,0:T(8,128)(2,1)} %bitcast.4, bf16[704,1408]{1,0:T(8,128)(2,1)} %bitcast.5, bf16[704,1408]{1,0:T(8,128)(2,1)} %bitcast.6, bf16[704,1408]{1,0:T(8,128)(2,1)} %wo_ref.1, ...), custom_call_target="tpu_custom_call" | custom-call | tf_op jit(solution)/shard_map/pallas_call | solution.py:267
  51.8 0.0 copy-start
  51.8 2.6 %copy.13 = bf16[32,16,1408]{2,1,0:T(8,128)(2,1)} copy(bf16[32,16,1408]{2,1,0:T(8,128)(2,1)} %get-tuple-element.4) | data formatting | bytes 2883584
  54.3 0.0 copy-done
  54.3 0.6 %copy.14 = f32[32,88]{1,0:T(8,128)} copy(f32[32,88]{1,0:T(8,128)S(1)} %copy-done) | data formatting | bytes 22528
Async XLA Ops:
  51.8 2.6 %copy-start = (f32[32,88]{1,0:T(8,128)S(1)}, f32[32,88]{1,0:T(8,128)}, u32[]{:S(2)}) copy-start(f32[32,88]{1,0:T(8,128)} %get-tuple-element.5) | copy-start | bytes 33796

commit v3 on v2

--- a/solution.py
+++ b/solution.py
@@ -10,6 +10,7 @@
 
 HEAD_SIZE = 88
 SLOTS = 4
+PIECES = 4
 LANES = 128
 MESH = pl.DeviceIdType.MESH
 F32 = jnp.float32
@@ -29,8 +30,8 @@
     x_ref, gain_ref, wq_ref, wk_ref, wv_ref, wo_ref, wd_ref, conv_ref, wu_ref,
     adapted_ref, pooled_ref,
     home, xr, normed, q, k, v, acc, att, ah, wq, wk, wv, wo, wd, wu,
-    block, red, halo, part, psend, precv,
-    load_sem, own_sem, x_send, x_recv, a_send, a_recv, h_send, h_recv, p_send, p_recv,
+    block, red, halo, out, part, psend, precv,
+    load_sem, own_sem, x_send, x_recv, a_send, a_recv, h_send, h_recv, p_send, p_recv, out_sem,
 ):
     f, p = lax.axis_index("frame"), lax.axis_index("patch")
     patches, width = x_ref.shape[1], x_ref.shape[2]
@@ -61,14 +62,14 @@
     home_copy = pltpu.make_async_copy(x_ref, home, own_sem.at[4])
 
     def x_copy(c, i):
-        d = lax.rem(p + i, n)
+        d = lax.rem(p + 9 * i, n)
         return pltpu.make_async_remote_copy(
             home.at[frame_of(c, d)], xr.at[c, i], x_send.at[c, i], x_recv.at[c, i],
             device_id=(f, d), device_id_type=MESH,
         )
 
     def a_copy(c, i):
-        d = lax.rem(p + n - i, n)
+        d = lax.rem(p + 9 * (n - i), n)
         return pltpu.make_async_remote_copy(
             att.at[c, i], ah.at[c, p], a_send.at[c, i], a_recv.at[c, p],
             device_id=(f, d), device_id_type=MESH,
@@ -92,7 +93,7 @@
     )
 
     def p_copy(i):
-        d = lax.rem(p + i, n)
+        d = lax.rem(p + 9 * i, n)
         return pltpu.make_async_remote_copy(
             psend.at[d], precv.at[i], p_send.at[i], p_recv.at[i],
             device_id=(f, d), device_id_type=MESH,
@@ -199,6 +200,8 @@
             block[start : start + half] = here[u * half : (u + 1) * half]
             red[1 + start : 1 + start + half] = reduced[u * half : (u + 1) * half]
 
+    out_copies = []
+
     def adapter(spans):
         taps = [
             jnp.concatenate([red[start + t : stop + t] for start, stop in spans]).astype(F32)
@@ -213,7 +216,9 @@
         for start, stop in spans:
             full = block[start:stop] + lifted[at : at + stop - start]
             part[start:stop, :] = jnp.sum(full, axis=1) / (n * patches)
-            adapted_ref[start:stop] = full.astype(BF16)
+            out[start:stop] = full.astype(BF16)
+            out_copies.append(pltpu.make_async_copy(out.at[start:stop], adapted_ref.at[start:stop], out_sem.at[len(out_copies)]))
+            out_copies[-1].start()
             at += stop - start
 
     come_home(0)
@@ -248,11 +253,50 @@
     def _(i):
         p_copy(i).wait_recv()
 
+    for copy in out_copies:
+        copy.wait()
     pooled_ref[...] = jnp.sum(precv[...].astype(F32), axis=0)[:, :share]
 
     @pl.loop(1, n)
     def _(i):
         p_copy(i).wait_send()
+
+
+def deliver_kernel(rows_ref, sums_ref, rows_out, sums_out, held, held_sums, sems):
+    step = rows_ref.shape[0] // PIECES
+    pieces = [
+        (rows_ref.at[pl.ds(i * step, step)], held.at[pl.ds(i * step, step)], rows_out.at[pl.ds(i * step, step)])
+        for i in range(PIECES)
+    ]
+    pieces.append((sums_ref, held_sums, sums_out))
+    reads = [pltpu.make_async_copy(a, b, sems.at[0, i]) for i, (a, b, _) in enumerate(pieces)]
+    writes = [pltpu.make_async_copy(b, c, sems.at[1, i]) for i, (_, b, c) in enumerate(pieces)]
+    for copy in reads:
+        copy.start()
+    for read, write in zip(reads, writes):
+        read.wait()
+        write.start()
+    for copy in writes:
+        copy.wait()
+
+
+def deliver(rows, sums):
+    anywhere = pl.BlockSpec(memory_space=pl.ANY)
+    return pl.pallas_call(
+        deliver_kernel,
+        out_shape=(
+            jax.ShapeDtypeStruct(rows.shape, rows.dtype),
+            jax.ShapeDtypeStruct(sums.shape, sums.dtype),
+        ),
+        in_specs=[anywhere, anywhere],
+        out_specs=(anywhere, anywhere),
+        scratch_shapes=[
+            pltpu.VMEM(rows.shape, rows.dtype),
+            pltpu.VMEM(sums.shape, sums.dtype),
+            pltpu.SemaphoreType.DMA((2, PIECES + 1)),
+        ],
+        compiler_params=pltpu.CompilerParams(vmem_limit_bytes=60 * 1024 * 1024),
+    )(rows, sums)
 
 
 def per_device(n, ring, frames_in, ln_gain, w_query, w_key, w_value, w_out, w_down, conv_kernel, w_up):
@@ -264,14 +308,14 @@
     vmem_spec = pl.BlockSpec(memory_space=pltpu.VMEM)
     dma = pltpu.SemaphoreType.DMA
     padded = -(-share // LANES) * LANES
-    return pl.pallas_call(
+    rows, sums = pl.pallas_call(
         functools.partial(layer_kernel, n, ring),
         out_shape=(
             jax.ShapeDtypeStruct((frames, patches, width), BF16),
             jax.ShapeDtypeStruct((frames, share), F32),
         ),
         in_specs=[any_spec, vmem_spec] + [any_spec] * 5 + [vmem_spec, any_spec],
-        out_specs=(vmem_spec, vmem_spec),
+        out_specs=(any_spec, vmem_spec),
         scratch_shapes=[
             pltpu.VMEM((frames, patches, width), BF16),
             pltpu.VMEM((2, n, patches, width), BF16),
@@ -291,11 +335,12 @@
             pltpu.VMEM((frames, patches, width), F32),
             pltpu.VMEM((frames + 2, patches, adapt), BF16),
             pltpu.VMEM((2, patches, adapt), BF16),
+            pltpu.VMEM((frames, patches, width), BF16),
             pltpu.VMEM((frames, width), F32),
             pltpu.VMEM((n, frames, padded), BF16),
             pltpu.VMEM((n, frames, padded), BF16),
             dma((6,)), dma((5,)), dma((2, n)), dma((2, n)), dma((2, n)), dma((2, n)),
-            dma((2,)), dma((2,)), dma((n,)), dma((n,)),
+            dma((2,)), dma((2,)), dma((n,)), dma((n,)), dma((5,)),
         ],
         compiler_params=pltpu.CompilerParams(
             collective_id=0, has_side_effects=True, vmem_limit_bytes=60 * 1024 * 1024
@@ -303,6 +348,7 @@
     )(
         frames_in, ln_gain, w_query.T, w_key.T, w_value.T, w_out, w_down.T, conv_kernel, w_up,
     )
+    return deliver(rows, sums)
 
 
 def solution(mesh):

time: 55.1 us -> 51.5 us (0.935)
  local copies, waits for them, and re-layouts: 3.18 us -> 0 us
    unnamed x4 -> x0, local copies, waits for them, and re-layouts: 3.18 us -> none
    pallas_call x1, Pallas kernels: 51.1 us -> 48.5 us  [per_device(): pl.pallas_call(functools.partial(layer_kernel, n, ring), out_shape=(jax.S...]
    pallas_call x0 -> x1, Pallas kernels: none -> 2.17 us  [deliver(): pl.pallas_call(deliver_kernel, out_shape=(jax.ShapeDtypeStruct(rows.shape...]
where the time goes in v3:
time: 51.5 us; the launch traced here: 51.3 us
  Pallas kernels  50.7 us (98%)
  between operations  0.64 us (1%)
    pallas_call x1, Pallas kernels, per_device(): pl.pallas_call(functools.partial(layer_kernel, n, ring), out_shape=(jax.S...  48.5 us
    pallas_call x1, Pallas kernels, deliver(): pl.pallas_call(deliver_kernel, out_shape=(jax.ShapeDtypeStruct(rows.shape...  2.17 us

profile of v3, /device:TPU:1, one launch (start us, length us, event | category | flops | bytes accessed | tf_op | source)
XLA Modules:
  0.0 51.3 jit_solution(16863444454742748974)
XLA Ops:
  0.6 48.5 %shard_map.104 = (bf16[32,16,1408]{2,1,0:T(8,128)(2,1)}, f32[32,88]{1,0:T(8,128)}) custom-call(bf16[32,16,1408]{2,1,0:T(8,128)(2,1)} %x_ref.1, f32[1408]{0:T(1024)} %gain_ref.1, bf16[704,1408]{1,0:T(8,128)(2,1)} %bitcast.4, bf16[704,1408]{1,0:T(8,128)(2,1)} %bitcast.5, bf16[704,1408]{1,0:T(8,128)(2,1)} %bitcast.6, bf16[704,1408]{1,0:T(8,128)(2,1)} %wo_ref.1, ...), custom_call_target="tpu_custom_call" | custom-call | tf_op jit(solution)/shard_map/pallas_call | solution.py:311
  49.2 2.2 %shard_map.105 = (bf16[32,16,1408]{2,1,0:T(8,128)(2,1)}, f32[32,88]{1,0:T(8,128)}) custom-call(bf16[32,16,1408]{2,1,0:T(8,128)(2,1)} %get-tuple-element.4.rows_ref, f32[32,88]{1,0:T(8,128)} %get-tuple-element.5.sums_ref), custom_call_target="tpu_custom_call" | custom-call | tf_op jit(solution)/shard_map/pallas_call | solution.py:285

commit v4 on v3

--- a/solution.py
+++ b/solution.py
@@ -177,7 +177,7 @@
 
         @pl.loop(1, n)
         def _(i):
-            a_copy(c, i).start()
+            a_copy(c, n - i).start()
 
     for load in loads[3:]:
         load.wait()
@@ -216,22 +216,31 @@
         for start, stop in spans:
             full = block[start:stop] + lifted[at : at + stop - start]
             part[start:stop, :] = jnp.sum(full, axis=1) / (n * patches)
-            out[start:stop] = full.astype(BF16)
-            out_copies.append(pltpu.make_async_copy(out.at[start:stop], adapted_ref.at[start:stop], out_sem.at[len(out_copies)]))
-            out_copies[-1].start()
+            block[start:stop] = full
             at += stop - start
+
+    def leave(spans):
+        for start, stop in spans:
+            out[start:stop] = block[start:stop].astype(BF16)
+            copy = pltpu.make_async_copy(out.at[start:stop], adapted_ref.at[start:stop], out_sem.at[len(out_copies)])
+            copy.start()
+            out_copies.append(copy)
+
+    early = [(1, half - 1), (last - half + 1, last - 1)]
+    late = [(0, 1), (half - 1, last - half + 1), (last - 1, last)]
 
     come_home(0)
     to_after.start()
     to_before.start()
-    adapter([(1, half - 1), (last - half + 1, last - 1)])
+    adapter(early)
+    leave(early)
 
     come_home(1)
     to_after.wait()
     to_before.wait()
     red[0] = jnp.where(f > 0, halo[0].astype(F32), 0.0).astype(BF16)
     red[last + 1] = jnp.where(f < ring - 1, halo[1].astype(F32), 0.0).astype(BF16)
-    adapter([(0, 1), (half - 1, last - half + 1), (last - 1, last)])
+    adapter(late)
 
     share = width // n
     for d in range(n):
@@ -242,6 +251,7 @@
         p_copy(i).start()
 
     precv[0] = psend[p]
+    leave(late)
 
     @pl.loop(1, n)
     def _(i):

time: 51.5 us -> 51.5 us (level)
  no operation moved by 1% of the time
where the time goes in v4:
time: 51.5 us; the launch traced here: 51.3 us
  Pallas kernels  50.6 us (98%)
  between operations  0.64 us (1%)
    pallas_call x1, Pallas kernels, per_device(): pl.pallas_call(functools.partial(layer_kernel, n, ring), out_shape=(jax.S...  48.5 us
    pallas_call x1, Pallas kernels, deliver(): pl.pallas_call(deliver_kernel, out_shape=(jax.ShapeDtypeStruct(rows.shape...  2.17 us

profile of v4, /device:TPU:1, one launch (start us, length us, event | category | flops | bytes accessed | tf_op | source)
XLA Modules:
  0.0 51.3 jit_solution(1336175668585591735)
XLA Ops:
  0.6 48.5 %shard_map.104 = (bf16[32,16,1408]{2,1,0:T(8,128)(2,1)}, f32[32,88]{1,0:T(8,128)}) custom-call(bf16[32,16,1408]{2,1,0:T(8,128)(2,1)} %x_ref.1, f32[1408]{0:T(1024)} %gain_ref.1, bf16[704,1408]{1,0:T(8,128)(2,1)} %bitcast.4, bf16[704,1408]{1,0:T(8,128)(2,1)} %bitcast.5, bf16[704,1408]{1,0:T(8,128)(2,1)} %bitcast.6, bf16[704,1408]{1,0:T(8,128)(2,1)} %wo_ref.1, ...), custom_call_target="tpu_custom_call" | custom-call | tf_op jit(solution)/shard_map/pallas_call | solution.py:321
  49.1 2.2 %shard_map.105 = (bf16[32,16,1408]{2,1,0:T(8,128)(2,1)}, f32[32,88]{1,0:T(8,128)}) custom-call(bf16[32,16,1408]{2,1,0:T(8,128)(2,1)} %get-tuple-element.4.rows_ref, f32[32,88]{1,0:T(8,128)} %get-tuple-element.5.sums_ref), custom_call_target="tpu_custom_call" | custom-call | tf_op jit(solution)/shard_map/pallas_call | solution.py:295
